TPU v7x, 32 devices: a whole 2x2x4 slice. The times are simulated.
32 devices in a mesh: section: 4 (over y, x), strip: 8 (over z, core).
Axes of the slice: x: 2, y: 2, z: 4, core: 2. Of those that a mesh axis runs over, the one named last changes fastest.
Arguments:
- images: bfloat16 [2, 32, 32, 256], P(None, 'strip'), may hold values from -6 to 6
- conv_first: bfloat16 [4, 9, 256, 256], P('section'), may hold values from -0.1875 to 0.1875
- conv_skip: bfloat16 [4, 9, 256, 256], P('section'), may hold values from -0.09375 to 0.09375
- conv_second: bfloat16 [4, 9, 256, 256], P('section'), may hold values from -0.1875 to 0.1875
- bias_first: float32 [4, 256], P('section'), may hold values from -0.8 to 0.8
- bias_second: float32 [4, 256], P('section'), may hold values from -0.8 to 0.8
Outputs:
- activations: bfloat16 [4, 2, 32, 32, 256], P('section', None, 'strip')
All inputs are finite; a program needn't handle non-finite values.
Results may differ from a plain program's by a relative error of at most 0.02.
Values may be sent and summed in bfloat16 or wider, within the bound.
A program may use at most 64 MiB of HBM per device.

v0:
```python
import functools

import jax
import jax.numpy as jnp
from jax import lax
from jax.experimental import pallas as pl
from jax.experimental.pallas import tpu as pltpu
from jax.sharding import PartitionSpec as P

MESH = pl.DeviceIdType.MESH
HALO = 2


def kernel(
    sections, strips,
    images, conv_first, conv_skip, conv_second, bias_first, bias_second,
    out,
    first_w, skip_w, second_w, first_b, second_b,
    land, skip_land, result, pre,
    weight_sem, image_sem, edge_send, land_recv, land_send, skip_recv, skip_send, out_sem,
):
    section = lax.axis_index("section")
    strip = lax.axis_index("strip")
    micro, rows, cols, channels = result.shape
    taps = 9 * channels
    middle = sections // 2
    is_first = section == 0
    has_next = section + 1 < sections
    has_above = strip > 0
    has_below = strip + 1 < strips
    sends_skip = (section > 0) & (section < middle)
    takes_skip = section > middle
    mirror = sections - section

    weights = (
        pltpu.make_async_copy(conv_first.at[0], first_w, weight_sem.at[0]),
        pltpu.make_async_copy(conv_second.at[0], second_w, weight_sem.at[1]),
        pltpu.make_async_copy(bias_first, first_b, weight_sem.at[2]),
        pltpu.make_async_copy(bias_second, second_b, weight_sem.at[3]),
    )
    skip_weight = pltpu.make_async_copy(conv_skip.at[0], skip_w, weight_sem.at[4])
    own_rows = pltpu.make_async_copy(images, land.at[:, pl.ds(HALO, rows)], image_sem)

    def pieces(source, target, m, to_section, send, recv):
        return (
            (None, pltpu.make_async_remote_copy(
                src_ref=source.at[m], dst_ref=target.at[m, pl.ds(HALO, rows)],
                send_sem=send.at[m, 0], recv_sem=recv.at[m, 0],
                device_id=(to_section, strip), device_id_type=MESH)),
            (has_above, pltpu.make_async_remote_copy(
                src_ref=source.at[m, pl.ds(0, HALO)], dst_ref=target.at[m, pl.ds(HALO + rows, HALO)],
                send_sem=send.at[m, 1], recv_sem=recv.at[m, 1],
                device_id=(to_section, strip - 1), device_id_type=MESH)),
            (has_below, pltpu.make_async_remote_copy(
                src_ref=source.at[m, pl.ds(rows - HALO, HALO)], dst_ref=target.at[m, pl.ds(0, HALO)],
                send_sem=send.at[m, 2], recv_sem=recv.at[m, 2],
                device_id=(to_section, strip + 1), device_id_type=MESH)),
        )

    def onward(m):
        return pieces(result, land, m, section + 1, land_send, land_recv)

    def skipped(m):
        return pltpu.make_async_remote_copy(
            src_ref=land.at[m], dst_ref=skip_land.at[m],
            send_sem=skip_send.at[m], recv_sem=skip_recv.at[m],
            device_id=(mirror, strip), device_id_type=MESH)

    def edges(m):
        return pieces(images, land, m, section, edge_send, land_recv)[1:]

    def start(group):
        for condition, copy in group:
            if condition is None:
                copy.start()
            else:
                pl.when(condition)(copy.start)

    def wait_sent(group):
        for condition, copy in group:
            if condition is None:
                copy.wait_send()
            else:
                pl.when(condition)(copy.wait_send)

    def wait_arrived(group):
        for condition, copy in group:
            if condition is None:
                copy.wait_recv()
            elif condition is has_above:
                pl.when(has_below)(copy.wait_recv)
            else:
                pl.when(has_above)(copy.wait_recv)

    for copy in weights:
        copy.start()
    pl.when(section >= middle)(skip_weight.start)
    pl.when(is_first)(own_rows.start)

    barrier = pltpu.get_barrier_semaphore()

    def greet_own(condition, to_section):
        @pl.when(condition)
        def _():
            pl.semaphore_signal(barrier, inc=1, device_id=(to_section, strip), device_id_type=MESH)

    def greet_beside(condition, to_section):
        @pl.when(condition)
        def _():
            @pl.when(has_above)
            def _():
                pl.semaphore_signal(barrier, inc=1, device_id=(to_section, strip - 1), device_id_type=MESH)

            @pl.when(has_below)
            def _():
                pl.semaphore_signal(barrier, inc=1, device_id=(to_section, strip + 1), device_id_type=MESH)

    greet_beside(is_first, section)
    greet_own(section > 0, section - 1)
    greet_beside(section > 0, section - 1)
    greet_own(takes_skip, mirror)

    beside = has_above.astype(jnp.int32) + has_below.astype(jnp.int32)
    expected = (
        jnp.where(is_first, beside, 0)
        + jnp.where(has_next, beside + 1, 0)
        + jnp.where(sends_skip, 1, 0)
    )
    @pl.when(expected > 0)
    def _():
        pl.semaphore_wait(barrier, expected)

    @pl.when(is_first)
    def _():
        for m in range(micro):
            start(edges(m))

    blank = jnp.zeros((micro, HALO, cols, channels), land.dtype)

    @pl.when(jnp.logical_not(has_above))
    def _():
        land[:, 0:HALO] = blank

    @pl.when(jnp.logical_not(has_below))
    def _():
        land[:, HALO + rows:] = blank

    pl.when(section >= middle)(skip_weight.wait)
    for copy in weights:
        copy.wait()

    @pl.when(section == middle)
    def _():
        def add(tap, carry):
            total = first_w[tap].astype(jnp.float32) + skip_w[tap].astype(jnp.float32)
            first_w[tap] = total.astype(first_w.dtype)
            return carry
        lax.fori_loop(0, 9, add, 0)

    pl.when(is_first)(own_rows.wait)

    def convolve(value, weight):
        in_rows = value.shape[0] // cols
        out_rows = in_rows - 2
        column = lax.rem(lax.broadcasted_iota(jnp.int32, value.shape, 0), cols)
        size = value.shape[0]
        left = jnp.where(column == 0, 0.0, pltpu.roll(value, 1, axis=0)).astype(jnp.bfloat16)
        centre = value.astype(jnp.bfloat16)
        right = jnp.where(column == cols - 1, 0.0, pltpu.roll(value, size - 1, axis=0)).astype(jnp.bfloat16)
        windows = [
            part[a * cols:(a + out_rows) * cols] for a in range(3) for part in (left, centre, right)
        ]
        return jnp.dot(
            jnp.concatenate(windows, axis=1),
            weight[...].reshape(taps, channels),
            preferred_element_type=jnp.float32,
        )

    def widened(buffer, m):
        return buffer[m].astype(jnp.float32).reshape((rows + 2 * HALO) * cols, channels)

    hidden_rows = rows + 2

    def step(m, carry):
        @pl.when(takes_skip)
        def _():
            skipped(m).wait_recv()
            pre[...] = convolve(widened(skip_land, m), skip_w) + first_b[...]

        @pl.when(jnp.logical_not(takes_skip))
        def _():
            pre[...] = jnp.broadcast_to(first_b[...], pre.shape)

        @pl.when(is_first)
        def _():
            wait_arrived(edges(m))

        @pl.when(section > 0)
        def _():
            wait_arrived(onward(m))

        hidden = jnp.maximum(convolve(widened(land, m), first_w) + pre[...], 0.0)
        row = lax.broadcasted_iota(jnp.int32, hidden.shape, 0)
        least = jnp.where(has_above, 0, cols)
        most = jnp.where(has_below, hidden_rows * cols, (hidden_rows - 1) * cols)
        hidden = jnp.where((row >= least) & (row < most), hidden, 0.0)
        final = jnp.maximum(convolve(hidden, second_w) + second_b[...], 0.0)
        result[m] = final.astype(jnp.bfloat16).reshape(rows, cols, channels)

        @pl.when(has_next)
        def _():
            start(onward(m))

        @pl.when(sends_skip)
        def _():
            skipped(m).start()

        pltpu.make_async_copy(result.at[m], out.at[0, m], out_sem.at[m]).start()
        return carry

    lax.fori_loop(0, micro, step, 0)

    for m in range(micro):
        pltpu.make_async_copy(result.at[m], out.at[0, m], out_sem.at[m]).wait()

        @pl.when(is_first)
        def _():
            wait_sent(edges(m))

        @pl.when(has_next)
        def _():
            wait_sent(onward(m))

        @pl.when(sends_skip)
        def _():
            skipped(m).wait_send()


def body(images, conv_first, conv_skip, conv_second, bias_first, bias_second):
    sections = lax.axis_size("section")
    strips = lax.axis_size("strip")
    micro, rows, cols, channels = images.shape
    padded = (micro, rows + 2 * HALO, cols, channels)
    weight = conv_first.shape[1:]
    copies = pltpu.SemaphoreType.DMA((micro, 3))
    pixels = rows * cols
    flops = 2 * micro * 2 * pixels * channels * channels * 9
    return pl.pallas_call(
        functools.partial(kernel, sections, strips),
        out_shape=jax.ShapeDtypeStruct((1, micro, rows, cols, channels), jnp.bfloat16),
        in_specs=[pl.BlockSpec(memory_space=pltpu.HBM)] * 6,
        out_specs=pl.BlockSpec(memory_space=pltpu.HBM),
        scratch_shapes=[
            pltpu.VMEM(weight, jnp.bfloat16),
            pltpu.VMEM(weight, jnp.bfloat16),
            pltpu.VMEM(weight, jnp.bfloat16),
            pltpu.VMEM((1, channels), jnp.float32),
            pltpu.VMEM((1, channels), jnp.float32),
            pltpu.VMEM(padded, jnp.bfloat16),
            pltpu.VMEM(padded, jnp.bfloat16),
            pltpu.VMEM((micro, rows, cols, channels), jnp.bfloat16),
            pltpu.VMEM(((rows + 2) * cols, channels), jnp.float32),
            pltpu.SemaphoreType.DMA((5,)),
            pltpu.SemaphoreType.DMA,
            copies, copies, copies,
            pltpu.SemaphoreType.DMA((micro,)),
            pltpu.SemaphoreType.DMA((micro,)),
            pltpu.SemaphoreType.DMA((micro,)),
        ],
        compiler_params=pltpu.CompilerParams(
            collective_id=0, has_side_effects=True, vmem_limit_bytes=32 * 1024 * 1024
        ),
        cost_estimate=pl.CostEstimate(
            flops=flops, bytes_accessed=3 * conv_first.size * 2, transcendentals=0
        ),
    )(images, conv_first, conv_skip, conv_second, bias_first, bias_second)


def solution(mesh):
    placed = (
        P(None, "strip", None, None),
        P("section", None, None, None),
        P("section", None, None, None),
        P("section", None, None, None),
        P("section", None),
        P("section", None),
    )
    return jax.shard_map(
        body,
        mesh=mesh,
        in_specs=placed,
        out_specs=P("section", None, "strip", None, None),
        check_vma=False,
    )
```

profile of v0, /device:TPU:23, one launch (start us, length us, event | category | flops | bytes accessed | tf_op | source)
XLA Modules:
  0.0 33.0 jit_solution(5107585433205731129)
XLA Ops:
  0.0 0.0 copy-start
  0.0 1.3 %copy-done = bf16[1,9,256,256]{3,2,1,0:T(8,128)(2,1)S(1)} copy-done((bf16[1,9,256,256]{3,2,1,0:T(8,128)(2,1)S(1)}, bf16[1,9,256,256]{3,2,1,0:T(8,128)(2,1)}, u32[]{:S(2)}) %copy-start) | copy-done | bytes 1179672
  1.3 0.0 copy-start.1
  1.3 1.3 %copy-done.1 = bf16[1,9,256,256]{3,2,1,0:T(8,128)(2,1)S(1)} copy-done((bf16[1,9,256,256]{3,2,1,0:T(8,128)(2,1)S(1)}, bf16[1,9,256,256]{3,2,1,0:T(8,128)(2,1)}, u32[]{:S(2)}) %copy-start.1) | copy-done | bytes 1179672
  2.5 0.0 copy-start.2
  2.5 1.3 %copy-done.2 = bf16[1,9,256,256]{3,2,1,0:T(8,128)(2,1)S(1)} copy-done((bf16[1,9,256,256]{3,2,1,0:T(8,128)(2,1)S(1)}, bf16[1,9,256,256]{3,2,1,0:T(8,128)(2,1)}, u32[]{:S(2)}) %copy-start.2) | copy-done | bytes 1179672
  3.8 0.0 copy-start.3
  3.8 0.9 %copy-done.3 = bf16[2,4,32,256]{3,2,1,0:T(8,128)(2,1)S(1)} copy-done((bf16[2,4,32,256]{3,2,1,0:T(8,128)(2,1)S(1)}, bf16[2,4,32,256]{3,2,1,0:T(8,128)(2,1)}, u32[]{:S(2)}) %copy-start.3) | copy-done | bytes 131096
  4.7 0.0 copy-start.4
  4.7 0.7 %copy-done.4 = f32[1,256]{1,0:T(1,128)S(1)} copy-done((f32[1,256]{1,0:T(1,128)S(1)}, f32[1,256]{1,0:T(1,128)}, u32[]{:S(2)}) %copy-start.4) | copy-done | bytes 1048
  5.4 0.0 copy-start.5
  5.4 0.7 %copy-done.5 = f32[1,256]{1,0:T(1,128)S(1)} copy-done((f32[1,256]{1,0:T(1,128)S(1)}, f32[1,256]{1,0:T(1,128)}, u32[]{:S(2)}) %copy-start.5) | copy-done | bytes 1048
  6.1 26.3 %shard_map.64 = bf16[1,2,4,32,256]{4,3,2,1,0:T(8,128)(2,1)S(1)} custom-call(bf16[2,4,32,256]{3,2,1,0:T(8,128)(2,1)S(1)} %copy-done.3, bf16[1,9,256,256]{3,2,1,0:T(8,128)(2,1)S(1)} %copy-done, bf16[1,9,256,256]{3,2,1,0:T(8,128)(2,1)S(1)} %copy-done.1, bf16[1,9,256,256]{3,2,1,0:T(8,128)(2,1)S(1)} %copy-done.2, f32[1,256]{1,0:T(1,128)S(1)} %copy-done.4, ...), custom_call_target="tpu_custom_call" | custom-call | flops 603979776 | bytes 3538944 | tf_op jit(solution)/shard_map/pallas_call | solution.py:248
  32.4 0.7 %copy.8 = bf16[1,2,4,32,256]{4,3,2,1,0:T(8,128)(2,1)} copy(bf16[1,2,4,32,256]{4,3,2,1,0:T(8,128)(2,1)S(1)} %shard_map.64) | data formatting | bytes 262144
Async XLA Ops:
  0.0 1.3 %copy-start = (bf16[1,9,256,256]{3,2,1,0:T(8,128)(2,1)S(1)}, bf16[1,9,256,256]{3,2,1,0:T(8,128)(2,1)}, u32[]{:S(2)}) copy-start(bf16[1,9,256,256]{3,2,1,0:T(8,128)(2,1)} %conv_first.1) | copy-start | bytes 3538948
  1.3 1.3 %copy-start.1 = (bf16[1,9,256,256]{3,2,1,0:T(8,128)(2,1)S(1)}, bf16[1,9,256,256]{3,2,1,0:T(8,128)(2,1)}, u32[]{:S(2)}) copy-start(bf16[1,9,256,256]{3,2,1,0:T(8,128)(2,1)} %conv_skip.1) | copy-start | bytes 3538948
  2.5 1.3 %copy-start.2 = (bf16[1,9,256,256]{3,2,1,0:T(8,128)(2,1)S(1)}, bf16[1,9,256,256]{3,2,1,0:T(8,128)(2,1)}, u32[]{:S(2)}) copy-start(bf16[1,9,256,256]{3,2,1,0:T(8,128)(2,1)} %conv_second.1) | copy-start | bytes 3538948
  3.8 0.9 %copy-start.3 = (bf16[2,4,32,256]{3,2,1,0:T(8,128)(2,1)S(1)}, bf16[2,4,32,256]{3,2,1,0:T(8,128)(2,1)}, u32[]{:S(2)}) copy-start(bf16[2,4,32,256]{3,2,1,0:T(8,128)(2,1)} %images.1) | copy-start | bytes 393220
  4.7 0.7 %copy-start.4 = (f32[1,256]{1,0:T(1,128)S(1)}, f32[1,256]{1,0:T(1,128)}, u32[]{:S(2)}) copy-start(f32[1,256]{1,0:T(1,128)} %bias_first.1) | copy-start | bytes 3076
  5.4 0.7 %copy-start.5 = (f32[1,256]{1,0:T(1,128)S(1)}, f32[1,256]{1,0:T(1,128)}, u32[]{:S(2)}) copy-start(f32[1,256]{1,0:T(1,128)} %bias_second.1) | copy-start | bytes 3076
where the time goes:
time: 33.3 us; the launch traced here: 33 us
  Pallas kernels  26.3 us (79%)
  local copies, waits for them, and re-layouts  6.73 us (20%)
    pallas_call x1, Pallas kernels, body(): pl.pallas_call(functools.partial(kernel, sections, strips), out_shape=jax...  26.3 us
    unnamed x13, local copies, waits for them, and re-layouts  6.73 us

commit v1 on v0

v1 whole, which is shorter than its diff:
```python
import functools

import jax
import jax.numpy as jnp
from jax import lax
from jax.experimental import pallas as pl
from jax.experimental.pallas import tpu as pltpu
from jax.sharding import PartitionSpec as P

MESH = pl.DeviceIdType.MESH
HALO = 2


def kernel(
    sections, strips,
    images, conv_first, conv_skip, conv_second, bias_first, bias_second,
    out,
    first_w, skip_w, second_w, first_b, second_b,
    land, skip_land, result, pre,
    weight_sem, image_sem, edge_send, edge_recv, land_send, land_recv, skip_send, skip_recv, out_sem,
):
    section = lax.axis_index("section")
    strip = lax.axis_index("strip")
    micro, rows, cols, channels = result.shape
    taps = 9 * channels
    middle = sections // 2
    is_first = section == 0
    has_next = section + 1 < sections
    has_above = strip > 0
    has_below = strip + 1 < strips
    sends_skip = (section > 0) & (section < middle)
    takes_skip = section > middle
    mirror = sections - section

    weights = (
        pltpu.make_async_copy(conv_first.at[0], first_w, weight_sem.at[0]),
        pltpu.make_async_copy(conv_second.at[0], second_w, weight_sem.at[1]),
        pltpu.make_async_copy(bias_first, first_b, weight_sem.at[2]),
        pltpu.make_async_copy(bias_second, second_b, weight_sem.at[3]),
    )
    skip_weight = pltpu.make_async_copy(conv_skip.at[0], skip_w, weight_sem.at[4])
    own_rows = pltpu.make_async_copy(images, land.at[:, pl.ds(HALO, rows)], image_sem)

    inner_below = lax.rem(strip, 2) == 0
    half = rows // 2
    outer_row = jnp.where(inner_below, 0, rows - half)
    inner_row = jnp.where(inner_below, rows - half, 0)

    def onward(m, part):
        row = (outer_row, inner_row)[part]
        return pltpu.make_async_remote_copy(
            src_ref=result.at[m, pl.ds(row, half)], dst_ref=land.at[m, pl.ds(HALO + row, half)],
            send_sem=land_send.at[m, part], recv_sem=land_recv.at[m, part],
            device_id=(section + 1, strip), device_id_type=MESH)

    def skipped(m):
        return pltpu.make_async_remote_copy(
            src_ref=land.at[m], dst_ref=skip_land.at[m],
            send_sem=skip_send.at[m], recv_sem=skip_recv.at[m],
            device_id=(mirror, strip), device_id_type=MESH)

    def upward(m):
        return pltpu.make_async_remote_copy(
            src_ref=land.at[m, pl.ds(HALO, HALO)], dst_ref=land.at[m, pl.ds(HALO + rows, HALO)],
            send_sem=edge_send.at[m, 0], recv_sem=edge_recv.at[m, 0],
            device_id=(section, strip - 1), device_id_type=MESH)

    def downward(m):
        return pltpu.make_async_remote_copy(
            src_ref=land.at[m, pl.ds(rows, HALO)], dst_ref=land.at[m, pl.ds(0, HALO)],
            send_sem=edge_send.at[m, 1], recv_sem=edge_recv.at[m, 1],
            device_id=(section, strip + 1), device_id_type=MESH)

    def pass_on(m, to_above, to_below):
        @pl.when(has_above & to_above)
        def _():
            upward(m).start()

        @pl.when(has_below & to_below)
        def _():
            downward(m).start()

    for copy in weights:
        copy.start()
    pl.when(section >= middle)(skip_weight.start)
    pl.when(is_first)(own_rows.start)

    barrier = pltpu.get_barrier_semaphore()

    def greet(condition, to_section, to_strip):
        @pl.when(condition)
        def _():
            pl.semaphore_signal(barrier, inc=1, device_id=(to_section, to_strip), device_id_type=MESH)

    greet(has_above, section, strip - 1)
    greet(has_below, section, strip + 1)
    greet(section > 0, section - 1, strip)
    greet(takes_skip, mirror, strip)
    expected = sum(
        condition.astype(jnp.int32) for condition in (has_above, has_below, has_next, sends_skip)
    )

    @pl.when(expected > 0)
    def _():
        pl.semaphore_wait(barrier, expected)

    @pl.when(is_first)
    def _():
        own_rows.wait()
        for m in range(micro):
            pass_on(m, True, True)

    blank = jnp.zeros((micro, HALO, cols, channels), land.dtype)

    @pl.when(jnp.logical_not(has_above))
    def _():
        land[:, 0:HALO] = blank

    @pl.when(jnp.logical_not(has_below))
    def _():
        land[:, HALO + rows:] = blank

    pl.when(section >= middle)(skip_weight.wait)
    for copy in weights:
        copy.wait()

    @pl.when(section == middle)
    def _():
        def add(tap, carry):
            total = first_w[tap].astype(jnp.float32) + skip_w[tap].astype(jnp.float32)
            first_w[tap] = total.astype(first_w.dtype)
            return carry
        lax.fori_loop(0, 9, add, 0)

    def convolve(value, weight):
        in_rows = value.shape[0]
        flat = value.reshape(in_rows * cols, channels)
        column = lax.broadcasted_iota(jnp.int32, value.shape, 1)

        def moved(distance, edge):
            rolled = pltpu.roll(flat, distance % (in_rows * cols), axis=0).reshape(value.shape)
            return jnp.where(column == edge, 0.0, rolled).astype(jnp.bfloat16)

        parts = (moved(1, 0), value.astype(jnp.bfloat16), moved(-1, cols - 1))
        windows = [
            part[a:a + in_rows - 2].reshape((in_rows - 2) * cols, channels)
            for a in range(3) for part in parts
        ]
        return jnp.dot(
            jnp.concatenate(windows, axis=1),
            weight[...].reshape(taps, channels),
            preferred_element_type=jnp.float32,
        )

    def widened(buffer, m):
        return buffer[m].astype(jnp.float32)

    hidden_rows = rows + 2

    def step(m, carry):
        @pl.when(takes_skip)
        def _():
            skipped(m).wait_recv()
            pre[...] = convolve(widened(skip_land, m), skip_w) + first_b[...]

        @pl.when(jnp.logical_not(takes_skip))
        def _():
            pre[...] = jnp.broadcast_to(first_b[...], pre.shape)

        @pl.when(section > 0)
        def _():
            onward(m, 0).wait_recv()
            pass_on(m, inner_below, jnp.logical_not(inner_below))
            onward(m, 1).wait_recv()
            pass_on(m, jnp.logical_not(inner_below), inner_below)

        @pl.when(has_below)
        def _():
            upward(m).wait_recv()

        @pl.when(has_above)
        def _():
            downward(m).wait_recv()

        hidden = jnp.maximum(convolve(widened(land, m), first_w) + pre[...], 0.0)
        hidden = hidden.reshape(hidden_rows, cols, channels)
        row = lax.broadcasted_iota(jnp.int32, hidden.shape, 0)
        least = jnp.where(has_above, 0, 1)
        most = jnp.where(has_below, hidden_rows, hidden_rows - 1)
        hidden = jnp.where((row >= least) & (row < most), hidden, 0.0)
        final = jnp.maximum(convolve(hidden, second_w) + second_b[...], 0.0)
        result[m] = final.astype(jnp.bfloat16).reshape(rows, cols, channels)

        @pl.when(has_next)
        def _():
            onward(m, 0).start()
            onward(m, 1).start()

        @pl.when(sends_skip)
        def _():
            skipped(m).start()

        pltpu.make_async_copy(result.at[m], out.at[0, m], out_sem.at[m]).start()
        return carry

    lax.fori_loop(0, micro, step, 0)

    for m in range(micro):
        pltpu.make_async_copy(result.at[m], out.at[0, m], out_sem.at[m]).wait()

        @pl.when(has_above)
        def _():
            upward(m).wait_send()

        @pl.when(has_below)
        def _():
            downward(m).wait_send()

        @pl.when(has_next)
        def _():
            onward(m, 0).wait_send()
            onward(m, 1).wait_send()

        @pl.when(sends_skip)
        def _():
            skipped(m).wait_send()


def body(images, conv_first, conv_skip, conv_second, bias_first, bias_second):
    sections = lax.axis_size("section")
    strips = lax.axis_size("strip")
    micro, rows, cols, channels = images.shape
    padded = (micro, rows + 2 * HALO, cols, channels)
    weight = conv_first.shape[1:]
    copies = pltpu.SemaphoreType.DMA((micro, 2))
    pixels = rows * cols
    flops = 2 * micro * 2 * pixels * channels * channels * 9
    return pl.pallas_call(
        functools.partial(kernel, sections, strips),
        out_shape=jax.ShapeDtypeStruct((1, micro, rows, cols, channels), jnp.bfloat16),
        in_specs=[pl.BlockSpec(memory_space=pltpu.HBM)] * 6,
        out_specs=pl.BlockSpec(memory_space=pltpu.HBM),
        scratch_shapes=[
            pltpu.VMEM(weight, jnp.bfloat16),
            pltpu.VMEM(weight, jnp.bfloat16),
            pltpu.VMEM(weight, jnp.bfloat16),
            pltpu.VMEM((1, channels), jnp.float32),
            pltpu.VMEM((1, channels), jnp.float32),
            pltpu.VMEM(padded, jnp.bfloat16),
            pltpu.VMEM(padded, jnp.bfloat16),
            pltpu.VMEM((micro, rows, cols, channels), jnp.bfloat16),
            pltpu.VMEM(((rows + 2) * cols, channels), jnp.float32),
            pltpu.SemaphoreType.DMA((5,)),
            pltpu.SemaphoreType.DMA,
            copies, copies, copies, copies,
            pltpu.SemaphoreType.DMA((micro,)),
            pltpu.SemaphoreType.DMA((micro,)),
            pltpu.SemaphoreType.DMA((micro,)),
        ],
        compiler_params=pltpu.CompilerParams(
            collective_id=0, has_side_effects=True
        ),
        cost_estimate=pl.CostEstimate(
            flops=flops, bytes_accessed=3 * conv_first.size * 2, transcendentals=0
        ),
    )(images, conv_first, conv_skip, conv_second, bias_first, bias_second)


def solution(mesh):
    placed = (
        P(None, "strip", None, None),
        P("section", None, None, None),
        P("section", None, None, None),
        P("section", None, None, None),
        P("section", None),
        P("section", None),
    )
    return jax.shard_map(
        body,
        mesh=mesh,
        in_specs=placed,
        out_specs=P("section", None, "strip", None, None),
        check_vma=False,
    )
```

time: 33.3 us -> 31 us (0.931)
  the two profiles are of different devices: /device:TPU:23 before, /device:TPU:15 now
where the time goes in v1:
time: 31 us; the launch traced here: 30.9 us
  Pallas kernels  29.3 us (95%)
  local copies, waits for them, and re-layouts  1.57 us (5%)
    pallas_call x1, Pallas kernels, body(): pl.pallas_call(functools.partial(kernel, sections, strips), out_shape=jax...  29.3 us
    unnamed x1, local copies, waits for them, and re-layouts  1.57 us

profile of v1, /device:TPU:15, one launch (start us, length us, event | category | flops | bytes accessed | tf_op | source)
XLA Modules:
  0.0 30.9 jit_solution(12591942723236293301)
XLA Ops:
  0.0 29.3 %shard_map.64 = bf16[1,2,4,32,256]{4,3,2,1,0:T(8,128)(2,1)} custom-call(bf16[2,4,32,256]{3,2,1,0:T(8,128)(2,1)} %images.1, bf16[1,9,256,256]{3,2,1,0:T(8,128)(2,1)} %conv_first.1, bf16[1,9,256,256]{3,2,1,0:T(8,128)(2,1)} %conv_skip.1, bf16[1,9,256,256]{3,2,1,0:T(8,128)(2,1)} %conv_second.1, f32[1,256]{1,0:T(1,128)} %bias_first.1, f32[1,256]{1,0:T(1,128)} %bias_second.1), custom_call_target="tpu_custom_call" | custom-call | flops 603979776 | bytes 3538944 | tf_op jit(solution)/shard_map/pallas_call | solution.py:238
  29.3 1.6 %copy.8 = bf16[1,2,4,32,256]{4,3,2,1,0:T(8,128)(2,1)} copy(bf16[1,2,4,32,256]{4,3,2,1,0:T(8,128)(2,1)} %shard_map.64) | data formatting | bytes 262144
